TPU v7x, 32 devices: a whole 2x2x4 slice. The times are simulated.
32 devices in a mesh: parts: 2 (over y), row: 4 (over z), col: 2 (over x), sub: 2 (over core).
Axes of the slice: x: 2, y: 2, z: 4, core: 2. Of those that a mesh axis runs over, the one named last changes fastest.
Arguments:
- ancestor_cov: float32 [64, 32, 256, 256], P(('parts', 'row'), 'col'), parts along dimension 0, may hold values from -6 to 6
- owner_slot: int32 [64], P('parts'), parts along dimension 0, may hold values from 0 to 31, each once
- parent_pattern: int32 [8, 12], P(('parts', 'sub')), parts along dimension 0, may hold values from 0 to 31, as said below
- parent_factor: float32 [8, 12, 256, 256], P(('parts', 'sub'), None, 'row'), parts along dimension 0, may hold values from -0.109375 to 0.109375
- parent_inverse: float32 [8, 256, 256], P(('parts', 'sub')), parts along dimension 0, may hold values from -6 to 6
- child_parent: int32 [8], P(('parts', 'sub')), parts along dimension 0, may hold values from 0 to 1
- child_pattern: int32 [8, 8], P(('parts', 'sub')), parts along dimension 0, may hold values from 0 to 11, as said below
- child_factor: float32 [8, 9, 256, 256], P(('parts', 'sub'), None, 'row'), parts along dimension 0, may hold values from -0.125 to 0.125
- child_inverse: float32 [8, 256, 256], P(('parts', 'sub')), parts along dimension 0, may hold values from -6 to 6
Outputs:
- parent_cov: float32 [8, 32, 256, 256], P(('parts', 'sub'), 'row'), parts along dimension 0
- parent_diag: float32 [8, 256, 256], P(('parts', 'sub')), parts along dimension 0
- child_cov: float32 [8, 32, 256, 256], P(('parts', 'sub'), 'row'), parts along dimension 0
- child_upper: float32 [8, 256, 256], P(('parts', 'sub')), parts along dimension 0
- child_diag: float32 [8, 256, 256], P(('parts', 'sub')), parts along dimension 0
There are 2 independent parts, one for each index of `parts`. A program takes and returns all parts, laid end to end along the dimension named above; each array names one. Nothing has to cross between parts.
Inputs may be any that keep to these rules, and one draw needn't show every extreme that they name: `parent_pattern`: each row holds distinct ancestor ids. `child_pattern`: each row holds distinct positions.
All inputs are finite; a program needn't handle non-finite values.
Results may differ from a plain program's by a relative error of at most 0.0001.
Values sent between devices are 32-bit elements; how exact they have to be, the bound alone decides.
No kernel may reach another device: no remote copies, remote signals or barrier semaphores. Data moves between devices by JAX's collectives and lax.ppermute only.
A program may use at most 192 MiB of HBM per device.

v0:
```python
import jax
import jax.numpy as jnp
from jax import lax
from jax.sharding import PartitionSpec as P

HIGH = lax.Precision.HIGHEST


def pick_rows(slot_list, targets):
    return (slot_list[:, None, :] == targets[None, :, None]).astype(jnp.float32)


def choose(selector, blocks):
    return jnp.einsum("jcp,jpxy->jcxy", selector, blocks, precision=HIGH)


def per_device(
    ancestor_cov,
    owner_slot,
    parent_pattern,
    parent_factor,
    parent_inverse,
    child_parent,
    child_pattern,
    child_factor,
    child_inverse,
):
    ancestor_count = owner_slot.shape[0]
    row_slots = ancestor_cov.shape[0]
    col_slots = ancestor_cov.shape[1]
    group_count = parent_pattern.shape[0]
    pattern_len = parent_pattern.shape[1]
    ancestor_ids = jnp.arange(ancestor_count, dtype=jnp.int32)
    match = (parent_pattern[:, :, None] == ancestor_ids[None, None, :]).astype(jnp.int32)
    slots = jnp.sum(match * owner_slot[None, None, :], axis=-1)
    row_ids = lax.axis_index("row") * row_slots + jnp.arange(row_slots, dtype=jnp.int32)
    col_ids = lax.axis_index("col") * col_slots + jnp.arange(col_slots, dtype=jnp.int32)
    parent_onehot = child_parent[:, None] == jnp.arange(group_count, dtype=jnp.int32)[None, :]
    kid_parent_slots = jnp.sum(
        parent_onehot[:, :, None].astype(jnp.int32) * slots[None, :, :], axis=1
    )
    rel_match = (
        child_pattern[:, :, None] == jnp.arange(pattern_len, dtype=jnp.int32)[None, None, :]
    ).astype(jnp.int32)
    kid_slots = jnp.sum(rel_match * kid_parent_slots[:, None, :], axis=-1)
    col_one = pick_rows(slots, col_ids)
    row_one = pick_rows(slots, row_ids)
    col_two = pick_rows(kid_slots, col_ids)
    row_two = pick_rows(kid_slots, row_ids)
    full_one, full_two = (
        lax.all_gather(parent_factor, "row", axis=2, tiled=True),
        lax.all_gather(child_factor, "row", axis=2, tiled=True),
    )
    wcol_one = choose(col_one, full_one)
    wrow_one = choose(row_one, full_one)
    lead = full_two[:, 0]
    wcol_two = choose(col_two, full_two[:, 1:])
    wrow_two = choose(row_two, full_two[:, 1:])
    mask_one = jnp.sum(row_one, axis=-1)
    mask_two = jnp.sum(row_two, axis=-1)
    parent_weight = parent_onehot.astype(jnp.float32)
    partial_one = jnp.einsum("icxy,jcyz->jixz", ancestor_cov, wcol_one, precision=HIGH)
    prod_one = lax.psum(partial_one, "col")
    parent_cov = -mask_one[:, :, None, None] * prod_one
    term_one = jnp.einsum("jixy,jixz->jyz", wrow_one, prod_one, precision=HIGH)
    parent_diag = parent_inverse - lax.psum(term_one, "row")
    kid_pcov = jnp.einsum("kj,jixy->kixy", parent_weight, parent_cov, precision=HIGH)
    partial_two = jnp.einsum("icxy,kcyz->kixz", ancestor_cov, wcol_two, precision=HIGH)
    prod_two = lax.psum(partial_two, "col")
    prod_two = prod_two + jnp.einsum("kixy,kyz->kixz", kid_pcov, lead, precision=HIGH)
    upper_part = jnp.einsum("kixy,kixz->kyz", kid_pcov, wrow_two, precision=HIGH)
    diag_part = jnp.einsum("kixy,kixz->kyz", wrow_two, prod_two, precision=HIGH)
    upper_sum, diag_sum = lax.psum((upper_part, diag_part), "row")
    kid_pdiag = jnp.einsum("kj,jxy->kxy", parent_weight, parent_diag, precision=HIGH)
    child_cov = -mask_two[:, :, None, None] * prod_two
    upper = jnp.einsum("kxy,kyz->kxz", kid_pdiag, lead, precision=HIGH) + upper_sum
    child_upper = -upper
    child_diag = child_inverse - jnp.einsum("kxy,kxz->kyz", lead, upper, precision=HIGH) - diag_sum
    return (parent_cov, parent_diag, child_cov, child_upper, child_diag)


def solution(mesh):
    in_specs = (
        P(("parts", "row"), "col", None, None),
        P("parts"),
        P(("parts", "sub"), None),
        P(("parts", "sub"), None, "row", None),
        P(("parts", "sub"), None, None),
        P(("parts", "sub")),
        P(("parts", "sub"), None),
        P(("parts", "sub"), None, "row", None),
        P(("parts", "sub"), None, None),
    )
    out_specs = (
        P(("parts", "sub"), "row", None, None),
        P(("parts", "sub"), None, None),
        P(("parts", "sub"), "row", None, None),
        P(("parts", "sub"), None, None),
        P(("parts", "sub"), None, None),
    )
    return jax.shard_map(
        per_device, mesh=mesh, in_specs=in_specs, out_specs=out_specs, check_vma=False
    )
```

profile of v0, /device:TPU:0, one launch (start us, length us, event | category | flops | bytes accessed | tf_op | source)
XLA Modules:
  0.0 643.6 jit_solution(5882674542085067443)
XLA Ops:
  11.1 35.0 %copy.54 = f32[8,16,256,256,1]{2,1,3,0,4:T(8,128)} copy(f32[8,16,256,256,1]{3,2,1,0,4:T(8,128)} %bitcast.92) | data formatting | bytes 67108864 | tf_op args[0]
  46.4 56.0 %all-gather.5.cloned.1.call-done = f32[2,9,256,256]{3,2,0,1:T(8,128)} async-done(((f32[2,9,64,256]{3,2,0,1:T(8,128)}), f32[2,9,256,256]{3,2,0,1:T(8,128)}) %all-gather.5.cloned.1.call-update) | async-done | bytes 4718608 | tf_op jit(solution)/shard_map/all_gather | solution.py:52
  102.3 2.6 slice.9
  107.1 5.8 fusion.12
  112.9 75.0 %fusion.22 = f32[2,8,256,256]{2,3,1,0:T(8,128)} fusion(f32[8,16,256,256,1]{2,1,3,0,4:T(8,128)} %copy.54, f32[2,16,256,256]{3,1,2,0:T(8,128)S(1)} %fusion.12), kind=kOutput, calls=%fused_computation.18 | convolution fusion | flops 51539607552 | bytes 46137344 | tf_op jit(solution)/shard_map/icxy,kcyz->kixz/dot_general | solution.py:68
  187.9 29.8 %all-gather.3.cloned.1.call-done = f32[2,12,256,256]{3,2,1,0:T(8,128)} async-done(((f32[2,12,64,256]{3,2,1,0:T(8,128)}), f32[2,12,256,256]{3,2,1,0:T(8,128)}) %all-gather.3.cloned.1.call-update) | async-done | bytes 6291472 | tf_op jit(solution)/shard_map/all_gather | solution.py:51
  217.7 10.7 %fusion.2 = f32[2,16,256,256]{3,1,2,0:T(8,128)S(1)} fusion(f32[2,12,256,256]{3,2,1,0:T(8,128)} %all-gather.3.cloned.1.call-done, s32[2,12]{1,0:T(2,128)S(1)} %copy.31, s32[16]{0:T(128)S(1)} %iota_add_fusion), kind=kOutput, calls=%fused_computation.2 | convolution fusion | flops 301990272 | bytes 14680224 | tf_op jit(solution)/shard_map/jcp,jpxy->jcxy/dot_general | solution.py:14
  228.4 62.6 %fusion.19 = f32[2,8,256,256]{2,3,1,0:T(8,128)} fusion(f32[8,16,256,256,1]{2,1,3,0,4:T(8,128)} %copy.54, f32[2,16,256,256]{3,1,2,0:T(8,128)S(1)} %fusion.2), kind=kOutput, calls=%fused_computation.17 | convolution fusion | flops 51539607552 | bytes 46137344 | tf_op jit(solution)/shard_map/icxy,jcyz->jixz/dot_general | solution.py:62
  291.8 8.7 %fusion.14 = f32[2,8,256,256]{3,1,2,0:T(8,128)} fusion(f32[2,8,256,256]{3,2,0,1:T(8,128)} %copy-done, s32[2,8]{1,0:T(2,128)S(1)} %copy-done.12, s32[8]{0:T(128)S(1)} %iota_add_fusion.1), kind=kOutput, calls=%fused_computation.14 | convolution fusion | flops 100663424 | bytes 8388704 | tf_op jit(solution)/shard_map/jcp,jpxy->jcxy/dot_general | solution.py:14
  300.5 7.4 %fusion = f32[2,8,256,256]{3,1,2,0:T(8,128)} fusion(f32[2,12,256,256]{3,2,1,0:T(8,128)S(1)} %bitcast.91, s32[2,12]{1,0:T(2,128)S(1)} %copy.31, s32[8]{0:T(128)S(1)} %iota_add_fusion.1), kind=kOutput, calls=%fused_computation | convolution fusion | flops 150995136 | bytes 10485888 | tf_op jit(solution)/shard_map/jcp,jpxy->jcxy/dot_general | solution.py:14
  307.9 180.0 %all-reduce.7.cloned.1.call-done = (f32[2,8,256,256]{2,3,1,0:T(8,128)}, f32[2,8,256,256]{2,3,1,0:T(8,128)}) async-done(((f32[2,8,256,256]{2,3,1,0:T(8,128)}, f32[2,8,256,256]{2,3,1,0:T(8,128)}), (f32[2,8,256,256]{2,3,1,0:T(8,128)}, f32[2,8,256,256]{2,3,1,0:T(8,128)})) %all-reduce.7.cloned.1.call-update) | async-done | bytes 8388624 | tf_op jit(solution)/shard_map/psum | solution.py:63
  487.8 5.4 copy.59
  493.3 4.7 broadcast_multiply_fusion.1
  498.0 7.3 %copy.36 = f32[2,8,256,256]{3,0,2,1:T(2,128)} copy(f32[2,8,256,256]{2,3,1,0:T(8,128)} %broadcast_multiply_fusion.1) | data formatting | bytes 8388608 | tf_op jit(solution)/shard_map/mul | solution.py:64
  505.3 10.2 %fusion.54 = f32[2,8,256,256]{3,0,2,1:T(2,128)S(1)} fusion(f32[2,8,256,256]{3,0,2,1:T(2,128)} %copy.36, s32[2]{0:T(128)S(1)} %copy-done.14), kind=kOutput, calls=%fused_computation.60 | convolution fusion | flops 25165828 | bytes 8388616 | tf_op jit(solution)/shard_map/kj,jixy->kixy/dot_general | solution.py:67
  515.5 7.9 %broadcast_multiply_fusion = (f32[2,8,256,256]{2,3,1,0:T(8,128)}, f32[2,8,256,256]{2,3,1,0:T(8,128)}) fusion(f32[2,8]{1,0:T(2,128)S(1)} %neg.20, f32[2,8,256,256]{2,3,1,0:T(8,128)S(1)} %copy-done.4, f32[2,9,256,256]{3,2,0,1:T(8,128)} %all-gather.5.cloned.1.call-done, f32[2,8,256,256]{3,0,2,1:T(2,128)S(1)} %fusion.54), kind=kOutput, calls=%fused_computation.19 | convolution fusion | flops 3223322624 | bytes 17301568 | tf_op jit(solution)/shard_map/kixy,kyz->kixz/dot_general | solution.py:70
  523.4 5.8 copy.76
  529.3 12.9 %fusion.27 = f32[2,256,256]{2,1,0:T(8,128)} fusion(f32[2,8,256,256]{3,1,2,0:T(8,128)} %fusion.14, f32[2,8,256,256]{3,0,2,1:T(2,128)} %copy-done.1), kind=kOutput, calls=%fused_computation.26 | convolution fusion | flops 3221225472 | bytes 8912896 | tf_op jit(solution)/shard_map/kixy,kixz->kyz/dot_general | solution.py:71
  542.2 8.0 %convolution_bitcast_fusion = f32[2,256,256]{1,2,0:T(8,128)} fusion(f32[2,8,256,256]{3,1,2,0:T(8,128)S(1)} %copy-done.2, f32[2,8,256,256]{3,1,2,0:T(8,128)S(1)} %copy-done.3), kind=kOutput, calls=%fused_computation.21 | convolution fusion | flops 3221225472 | bytes 8912896 | tf_op jit(solution)/shard_map/kixy,kixz->kyz/dot_general | solution.py:72
  550.3 7.9 %convolution_bitcast_fusion.2 = f32[2,256,256]{2,1,0:T(8,128)} fusion(f32[2,8,256,256]{3,1,2,0:T(8,128)S(1)} %copy-done.5, f32[2,8,256,256]{3,1,2,0:T(8,128)S(1)} %copy-done.6), kind=kOutput, calls=%fused_computation.27 | convolution fusion | flops 3221225472 | bytes 8912896 | tf_op jit(solution)/shard_map/jixy,jixz->jyz/dot_general | solution.py:65
  558.4 5.4 copy.47
  563.8 5.6 copy.48
  569.4 59.2 %all-reduce.5.cloned.1.call-done = (f32[2,256,256]{2,1,0:T(8,128)}, f32[2,256,256]{2,1,0:T(8,128)}, f32[2,256,256]{1,2,0:T(8,128)}) async-done(((f32[2,256,256]{2,1,0:T(8,128)}, f32[2,256,256]{2,1,0:T(8,128)}, f32[2,256,256]{1,2,0:T(8,128)}), (f32[2,256,256]{2,1,0:T(8,128)}, f32[2,256,256]{2,1,0:T(8,128)}, f32[2,256,256]{1,2,0:T(8,128)})) %all-reduce.5.cloned.1.call-update) | async-done | bytes 1572880 | tf_op jit(solution)/shard_map/psum | solution.py:66
  631.1 2.7 fusion.60
  (67 shorter events, 12.8 us)
Async XLA Ops:
  7.2 3.3 copy-start.15
  7.2 3.4 copy-start.17
  7.2 3.8 copy-start.13
  7.2 95.1 %all-gather.5.cloned.1.call-start = ((), (), s32[]{:S(2)}) async-start(), calls=%async_computation.1 | async-start | bytes 5898240 | tf_op jit(solution)/shard_map/all_gather | solution.py:52
  9.7 208.0 %all-gather.3.cloned.1.call-start = ((), (), s32[]{:S(2)}) async-start(), calls=%async_computation | async-start | bytes 7864320 | tf_op jit(solution)/shard_map/all_gather | solution.py:51
  10.4 477.4 %all-reduce.7.cloned.1.call-start = ((), (), s32[]{:S(2)}) async-start(), calls=%async_computation.3 | async-start | bytes 16777216 | tf_op jit(solution)/shard_map/psum | solution.py:63
  11.1 35.0 %copy-start.16 = (s32[2,8]{1,0:T(2,128)S(1)}, s32[2,8]{1,0:T(2,128)}, u32[]{:S(2)}) copy-start(s32[2,8]{1,0:T(2,128)} %param.15) | copy-start | bytes 196
  46.3 58.6 %copy-start.11 = (s32[2,8]{1,0:T(2,128)}, s32[2,8]{1,0:T(2,128)S(1)}, u32[]{:S(2)}) copy-start(s32[2,8]{1,0:T(2,128)S(1)} %select_reduce_fusion) | copy-start | bytes 196
  105.0 2.1 copy-start
  290.9 0.7 copy-start.12
  290.9 9.6 %slice-start = ((s8[6291456]{0:T(1024)(128)(4,1)}), s8[2097152]{0:T(1024)(128)(4,1)S(1)}, s32[]{:S(2)}) async-start(s8[6291456]{0:T(1024)(128)(4,1)} %bitcast.90), calls=%async_computation.4 | async-start | bytes 4194304
  291.0 337.6 %all-reduce.5.cloned.1.call-start = ((), (), s32[]{:S(2)}) async-start(), calls=%async_computation.2 | async-start | bytes 3145728 | tf_op jit(solution)/shard_map/psum | solution.py:66
  291.0 9.5 %slice-start.1 = ((s8[6291456]{0:T(1024)(128)(4,1)}), s8[4194304]{0:T(1024)(128)(4,1)S(1)}, s32[]{:S(2)}) async-start(s8[6291456]{0:T(1024)(128)(4,1)} %bitcast.90), calls=%async_computation.5 | async-start | bytes 8388608
  498.0 7.3 %copy-start.14 = (s32[2]{0:T(128)S(1)}, s32[2]{0:T(128)}, u32[]{:S(2)}) copy-start(s32[2]{0:T(128)} %param.14) | copy-start | bytes 28
  505.3 10.3 %copy-start.4 = (f32[2,8,256,256]{2,3,1,0:T(8,128)S(1)}, f32[2,8,256,256]{2,3,1,0:T(8,128)}, u32[]{:S(2)}) copy-start(f32[2,8,256,256]{2,3,1,0:T(8,128)} %get-tuple-element.19) | copy-start | bytes 12582916
  515.5 7.9 %copy-start.1 = (f32[2,8,256,256]{3,0,2,1:T(2,128)}, f32[2,8,256,256]{3,0,2,1:T(2,128)S(1)}, u32[]{:S(2)}) copy-start(f32[2,8,256,256]{3,0,2,1:T(2,128)S(1)} %fusion.54) | copy-start | bytes 12582916
  529.3 13.0 %copy-start.2 = (f32[2,8,256,256]{3,1,2,0:T(8,128)S(1)}, f32[2,8,256,256]{3,1,2,0:T(8,128)}, u32[]{:S(2)}) copy-start(f32[2,8,256,256]{3,1,2,0:T(8,128)} %fusion.14) | copy-start | bytes 12582916
  529.3 12.9 %copy-start.3 = (f32[2,8,256,256]{3,1,2,0:T(8,128)S(1)}, f32[2,8,256,256]{3,1,2,0:T(8,128)}, u32[]{:S(2)}) copy-start(f32[2,8,256,256]{3,1,2,0:T(8,128)} %copy.76) | copy-start | bytes 12582916
  542.2 8.0 %copy-start.5 = (f32[2,8,256,256]{3,1,2,0:T(8,128)S(1)}, f32[2,8,256,256]{3,1,2,0:T(8,128)}, u32[]{:S(2)}) copy-start(f32[2,8,256,256]{3,1,2,0:T(8,128)} %fusion) | copy-start | bytes 12582916
  542.2 8.0 %copy-start.6 = (f32[2,8,256,256]{3,1,2,0:T(8,128)S(1)}, f32[2,8,256,256]{3,1,2,0:T(8,128)}, u32[]{:S(2)}) copy-start(f32[2,8,256,256]{3,1,2,0:T(8,128)} %copy.59) | copy-start | bytes 12582916
  550.3 7.9 %copy-start.10 = (f32[2,256,256]{2,1,0:T(8,128)S(1)}, f32[2,256,256]{2,1,0:T(8,128)}, u32[]{:S(2)}) copy-start(f32[2,256,256]{2,1,0:T(8,128)} %param.17) | copy-start | bytes 1572868
  563.8 64.8 %copy-start.8 = (f32[2,256,256]{2,1,0:T(8,128)S(1)}, f32[2,256,256]{2,1,0:T(8,128)}, u32[]{:S(2)}) copy-start(f32[2,256,256]{2,1,0:T(8,128)} %param.13) | copy-start | bytes 1572868
  628.6 5.2 copy-start.9
  629.8 7.1 %copy-start.7 = (f32[2,256,256]{2,1,0:T(8,128)}, f32[2,256,256]{2,1,0:T(8,128)S(1)}, u32[]{:S(2)}) copy-start(f32[2,256,256]{2,1,0:T(8,128)S(1)} %sub.9) | copy-start | bytes 1572868
Sparse Core Ops, SparseCore 0:
  10.2 92.0 all-gather.4
  103.9 113.7 all-gather.2
  291.1 196.7 all-reduce.6
  558.3 70.2 all-reduce.4
where the time goes:
time: 650 us; the launch traced here: 644 us
  waiting for transfers between devices  326 us (50%)
  matrix products  223 us (34%)
  local copies, waits for them, and re-layouts  73.5 us (11%)
  between operations  14.3 us (2%)
  other arithmetic  6.93 us (1%)
    psum x1, waiting for transfers between devices, per_device(): prod_one = lax.psum(partial_one, 'col')  180 us
    dot_general x1, matrix products, per_device(): jnp.einsum('icxy,kcyz->kixz', ancestor_cov, wcol_two, precision=HIGH)  75 us
    dot_general x1, matrix products, per_device(): jnp.einsum('icxy,jcyz->jixz', ancestor_cov, wcol_one, precision=HIGH)  62.6 us
    psum x1, waiting for transfers between devices, per_device(): parent_diag = parent_inverse - lax.psum(term_one, 'row')  59.2 us
    all_gather x1, waiting for transfers between devices, per_device(): lax.all_gather(child_factor, 'row', axis=2, tiled=True)  56 us
    unnamed x47, local copies, waits for them, and re-layouts  52.2 us
    dot_general x4, matrix products, choose(): return jnp.einsum('jcp,jpxy->jcxy', selector, blocks, precision=HIGH)  32.5 us
    all_gather x1, waiting for transfers between devices, per_device(): lax.all_gather(parent_factor, 'row', axis=2, tiled=True)  29.8 us
  transfers between devices with their start and end apart: 4, of which 4 were waited for; matrix products, arithmetic and copies ran while one was open for 23% of the time, Pallas kernels for 0%

commit v1 on v0

v1 whole, which is shorter than its diff:
```python
import functools

import jax
import jax.numpy as jnp
from jax import lax
from jax.experimental import pallas as pl
from jax.experimental.pallas import tpu as pltpu
from jax.sharding import PartitionSpec as P

HIGH = lax.Precision.HIGHEST
VMEM_LIMIT = 50 * 1024 * 1024
SLACK = 4
DEPTH = 8
SMEM = pl.BlockSpec(memory_space=pltpu.SMEM)
VMEM = pl.BlockSpec(memory_space=pltpu.VMEM)
HBM = pl.BlockSpec(memory_space=pl.ANY)


class Layout:
    def __init__(self, count, length, lead, row_slots, col_slots, rows, cols):
        self.count, self.length, self.lead = count, length, lead
        self.row_slots, self.col_slots, self.rows, self.cols = row_slots, col_slots, rows, cols
        total = count * length
        self.full_w = total + lead
        self.cap_w = min(total, -(-total // cols) + SLACK) + lead
        self.full_y = count * min(length, row_slots)
        self.cap_y = min(self.full_y, -(-total // rows) + SLACK)
        products = self.full_y * min(length, col_slots)
        self.y_at = 4
        self.out_at = self.y_at + 4 * self.full_y
        self.a_at = self.out_at + count * row_slots
        self.w_at = self.a_at + products
        self.p_at = self.w_at + products
        self.size = self.p_at + products


def plan_kernel(lay, upper, here, owner, parents, kid_parent, kid_pattern, factor, tab, most, send, spill, *scratch):
    col_count, row_count, at_block, sems = scratch
    row, col = here[0], here[1]
    held = send.shape[0]
    for i in range(lay.cols):
        col_count[i] = 0
    for i in range(lay.rows):
        row_count[i] = 0

    def clear(i, _):
        tab[lay.out_at + i] = -1
        return 0

    lax.fori_loop(0, lay.count * lay.row_slots, clear, 0)

    def copy_to(target, source, place):
        return pltpu.make_async_copy(factor.at[source // (lay.length + upper_lead), source % (lay.length + upper_lead)], target, sems.at[place])

    upper_lead = 1 if lay.lead else 0
    for m in range(lay.lead):
        copy_to(send.at[m], m * (lay.length + 1), m).start()
    blocks, listed, products = jnp.int32(lay.lead), jnp.int32(0), jnp.int32(0)
    for m in range(lay.count):
        first_block, first_row = blocks, listed
        parent = m if upper else kid_parent[m]

        def visit(p, carry):
            blocks, listed = carry
            slot = owner[parents[m, p]] if upper else owner[parents[parent, kid_pattern[m, p]]]
            slot_col, slot_row = slot // lay.col_slots, slot // lay.row_slots
            col_count[slot_col] = col_count[slot_col] + 1
            row_count[slot_row] = row_count[slot_row] + 1
            mine_col, mine_row = slot_col == col, slot_row == row
            source = m * (lay.length + upper_lead) + p + upper_lead

            @pl.when(mine_col)
            def _():
                at_block[blocks] = slot - col * lay.col_slots

                @pl.when(blocks < held)
                def _():
                    copy_to(send.at[blocks], source, blocks).start()

                if spill is not None:

                    @pl.when(blocks >= held)
                    def _():
                        copy_to(spill.at[blocks - held], source, blocks).start()

            @pl.when(mine_row)
            def _():
                local = slot - row * lay.row_slots
                base = lay.y_at + 4 * listed
                tab[base] = m
                tab[base + 1] = local
                tab[base + 2] = jnp.where(mine_col, blocks, -1)
                tab[base + 3] = parent
                tab[lay.out_at + m * lay.row_slots + local] = listed

            return blocks + mine_col.astype(jnp.int32), listed + mine_row.astype(jnp.int32)

        blocks, listed = lax.fori_loop(0, lay.length, visit, (blocks, listed))

        def each_row(y, count):
            local = tab[lay.y_at + 4 * y + 1]

            def each_block(w, count):
                tab[lay.a_at + count] = local * lay.col_slots + at_block[w]
                tab[lay.w_at + count] = w
                tab[lay.p_at + count] = y
                return count + 1

            return lax.fori_loop(first_block, blocks, each_block, count)

        products = lax.fori_loop(first_row, listed, each_row, products)
    tab[0] = products
    tab[1] = listed
    tab[2] = blocks
    tab[3] = 0
    most_col, most_row = col_count[0], row_count[0]
    for i in range(1, lay.cols):
        most_col = jnp.maximum(most_col, col_count[i])
    for i in range(1, lay.rows):
        most_row = jnp.maximum(most_row, row_count[i])
    most[0] = most_col + lay.lead
    most[1] = most_row

    def land(i, _):
        copy_to(send.at[0], 0, i).wait()
        return 0

    lax.fori_loop(0, blocks, land, 0)


def plan(lay, upper, here, owner, parents, kid_parent, kid_pattern, factor):
    block = factor.shape[2:]
    spilled = lay.full_w - lay.cap_w
    outs = [
        jax.ShapeDtypeStruct((lay.size,), jnp.int32),
        jax.ShapeDtypeStruct((2,), jnp.int32),
        jax.ShapeDtypeStruct((lay.cap_w,) + block, jnp.float32),
    ]
    specs = [SMEM, SMEM, HBM]
    if spilled:
        outs.append(jax.ShapeDtypeStruct((spilled,) + block, jnp.float32))
        specs.append(HBM)

    def body(*refs):
        refs = list(refs)
        if not spilled:
            refs.insert(9, None)
        plan_kernel(lay, upper, *refs)

    got = pl.pallas_call(
        body,
        out_shape=outs,
        in_specs=[SMEM] * 5 + [HBM],
        out_specs=specs,
        scratch_shapes=[
            pltpu.SMEM((lay.cols,), jnp.int32),
            pltpu.SMEM((lay.rows,), jnp.int32),
            pltpu.SMEM((lay.full_w,), jnp.int32),
            pltpu.SemaphoreType.DMA((lay.full_w,)),
        ],
        compiler_params=pltpu.CompilerParams(vmem_limit_bytes=VMEM_LIMIT),
    )(here, owner, parents, kid_parent, kid_pattern, factor)
    return got if spilled else list(got) + [None]


def halves(x):
    high = x.astype(jnp.bfloat16)
    return high, (x - high.astype(jnp.float32)).astype(jnp.bfloat16)


def dot3(a, b, dims):
    f = functools.partial(lax.dot_general, dimension_numbers=(dims, ((), ())), preferred_element_type=jnp.float32)
    return f(a[0], b[0]) + (f(a[0], b[1]) + f(a[1], b[0]))


PLAIN = ((1,), (0,))
TURNED = ((0,), (0,))


def mult_kernel(lay, pieces, here, tab, ancestors, *refs):
    bufs, (y, w, high, low, slots, w_sems, a_sems) = refs[: lay.rows * pieces], refs[lay.rows * pieces :]
    row = here[0]
    copies = []
    for piece in range(pieces):
        start = 0 if piece == 0 else lay.cap_w
        for k in range(lay.rows):
            buf = bufs[piece * lay.rows + k]
            depth = buf.shape[1]
            owner = lax.rem(row - k + lay.rows, lay.rows)
            target = w.at[pl.ds(start, buf.shape[0]), pl.ds(pl.multiple_of(owner * depth, depth), depth), :]
            copies.append(pltpu.make_async_copy(buf, target, w_sems.at[piece * lay.rows + k]))
    for copy in copies:
        copy.start()
    products, blocks = tab[0], tab[2]

    def fetch(i):
        block = tab[lay.a_at + i]
        source = ancestors.at[block // lay.col_slots, block % lay.col_slots]
        return pltpu.make_async_copy(source, slots.at[lax.rem(i, DEPTH)], a_sems.at[lax.rem(i, DEPTH)])

    def fetch_next(i):
        @pl.when(i < products)
        def _():
            fetch(i).start()

    for i in range(DEPTH - 1):
        fetch_next(jnp.int32(i))
    y[...] = jnp.zeros_like(y)
    for copy in copies:
        copy.wait()

    def split(i, _):
        high[i], low[i] = halves(w[i])
        return 0

    lax.fori_loop(lay.lead, blocks, split, 0)

    def step(i, _):
        fetch_next(i + DEPTH - 1)
        fetch(i).wait()
        at, to = tab[lay.w_at + i], tab[lay.p_at + i]
        y[to] += dot3(halves(slots[lax.rem(i, DEPTH)]), (high[at], low[at]), PLAIN)
        return 0

    lax.fori_loop(0, products, step, 0)


def mult(lay, cap_w, cap_y, here, tab, ancestors, bufs):
    size = ancestors.shape[2]
    pieces = len(bufs) // lay.rows
    return pl.pallas_call(
        functools.partial(mult_kernel, lay, pieces),
        out_shape=[
            jax.ShapeDtypeStruct((cap_y, size, size), jnp.float32),
            jax.ShapeDtypeStruct((cap_w, size, size), jnp.float32),
        ],
        in_specs=[SMEM, SMEM, HBM] + [HBM] * len(bufs),
        out_specs=[VMEM, VMEM],
        scratch_shapes=[
            pltpu.VMEM((cap_w, size, size), jnp.bfloat16),
            pltpu.VMEM((cap_w, size, size), jnp.bfloat16),
            pltpu.VMEM((DEPTH, size, size), jnp.float32),
            pltpu.SemaphoreType.DMA((len(bufs),)),
            pltpu.SemaphoreType.DMA((DEPTH,)),
        ],
        compiler_params=pltpu.CompilerParams(vmem_limit_bytes=VMEM_LIMIT),
        cost_estimate=pl.CostEstimate(flops=10**9, bytes_accessed=2 * 10**7, transcendentals=0),
    )(here, tab, ancestors, *bufs)


def spread_kernel(lay, extra, tab, own, other, w, *refs):
    add, (cov, term) = (refs[0], refs[1:]) if extra else (None, refs)
    term[...] = jnp.zeros_like(term)
    for m in range(lay.count):
        for s in range(lay.row_slots):
            place = tab[lay.out_at + m * lay.row_slots + s]

            @pl.when(place < 0)
            def _():
                cov[m, s] = jnp.zeros(cov.shape[2:], jnp.float32)

    def step(y, _):
        base = lay.y_at + 4 * y
        m, s, at = tab[base], tab[base + 1], tab[base + 2]
        total = own[y] + other[y]
        if extra:
            total = total + add[y]
        cov[m, s] = -total

        @pl.when(at >= 0)
        def _():
            term[m] += dot3(halves(w[at]), halves(total), TURNED)

        return 0

    lax.fori_loop(0, tab[1], step, 0)


def spread(lay, tab, own, other, w, add=None):
    size = own.shape[1]
    more = [] if add is None else [add]
    return pl.pallas_call(
        functools.partial(spread_kernel, lay, add is not None),
        out_shape=[
            jax.ShapeDtypeStruct((lay.count, lay.row_slots, size, size), jnp.float32),
            jax.ShapeDtypeStruct((lay.count, size, size), jnp.float32),
        ],
        in_specs=[SMEM] + [VMEM] * (3 + len(more)),
        out_specs=[VMEM, VMEM],
        compiler_params=pltpu.CompilerParams(vmem_limit_bytes=VMEM_LIMIT),
        cost_estimate=pl.CostEstimate(flops=10**9, bytes_accessed=10**7, transcendentals=0),
    )(tab, own, other, w, *more)


def cross_kernel(lay, tab, cov, w, through, upper):
    upper[...] = jnp.zeros_like(upper)

    def step(y, _):
        base = lay.y_at + 4 * y
        m, s, at, parent = tab[base], tab[base + 1], tab[base + 2], tab[base + 3]
        block = halves(cov[parent, s])
        through[y] = dot3(block, halves(w[m]), PLAIN)

        @pl.when(at >= 0)
        def _():
            upper[m] += dot3(block, halves(w[at]), TURNED)

        return 0

    lax.fori_loop(0, tab[1], step, 0)


def cross(lay, cap_y, tab, cov, w):
    size = w.shape[1]
    return pl.pallas_call(
        functools.partial(cross_kernel, lay),
        out_shape=[
            jax.ShapeDtypeStruct((cap_y, size, size), jnp.float32),
            jax.ShapeDtypeStruct((lay.count, size, size), jnp.float32),
        ],
        in_specs=[SMEM, VMEM, VMEM],
        out_specs=[VMEM, VMEM],
        compiler_params=pltpu.CompilerParams(vmem_limit_bytes=VMEM_LIMIT),
        cost_estimate=pl.CostEstimate(flops=10**9, bytes_accessed=10**7, transcendentals=0),
    )(tab, cov, w)


def shift(x, axis, size, by):
    return lax.ppermute(x, axis, [(i, (i + by) % size) for i in range(size)])


def ring(x, rows):
    out = [x]
    for _ in range(rows - 1):
        out.append(shift(out[-1], "row", rows, 1))
    return out


def other_half(x, cols):
    if cols == 2:
        return shift(x, "col", 2, 1)
    return lax.psum(x, "col") - x


def total(x, rows, cols):
    if cols != 2 or x.shape[0] != 2 or rows > 4:
        return lax.psum(x, ("row", "col"))
    row, col = lax.axis_index("row"), lax.axis_index("col")
    mine = lax.dynamic_index_in_dim(x, col, 0, False) + shift(lax.dynamic_index_in_dim(x, 1 - col, 0, False), "col", 2, 1)
    parts = mine.reshape(rows, -1, mine.shape[1])
    chunk = lax.dynamic_index_in_dim(parts, row, 0, False)
    arrived = [
        shift(lax.dynamic_index_in_dim(parts, lax.rem(row + d, rows), 0, False), "row", rows, d) for d in range(1, rows)
    ]
    for piece in arrived:
        chunk = chunk + piece
    pieces = [chunk] + [shift(chunk, "row", rows, d) for d in range(1, rows)]
    ordered = jnp.stack(pieces[::-1])
    mine = jnp.concatenate([ordered, ordered])
    mine = lax.dynamic_slice_in_dim(mine, rows - 1 - row, rows, 0).reshape(x.shape[1:])
    theirs = shift(mine, "col", 2, 1)
    return jnp.stack([jnp.where(col == 0, mine, theirs), jnp.where(col == 0, theirs, mine)])


def per_device(
    rows,
    cols,
    others,
    ancestor_cov,
    owner_slot,
    parent_pattern,
    parent_factor,
    parent_inverse,
    child_parent,
    child_pattern,
    child_factor,
    child_inverse,
):
    row_slots, col_slots = ancestor_cov.shape[:2]
    up = Layout(*parent_pattern.shape, 0, row_slots, col_slots, rows, cols)
    low = Layout(*child_pattern.shape, child_pattern.shape[0], row_slots, col_slots, rows, cols)
    here = jnp.stack([lax.axis_index("row"), lax.axis_index("col")]).astype(jnp.int32)
    index = (here, owner_slot, parent_pattern, child_parent, child_pattern)
    up_tab, up_most, up_send, up_spill = plan(up, True, *index, parent_factor)
    low_tab, low_most, low_send, low_spill = plan(low, False, *index, child_factor)
    up_bufs = ring(up_send, rows)
    most = jnp.concatenate([up_most, low_most])
    for axis, size in others:
        seen = most
        for by in range(1, size):
            most = jnp.maximum(most, shift(seen, axis, size, by))
    limits = (up.cap_w, up.cap_y, low.cap_w, low.cap_y)
    over = jnp.any(most > jnp.array(limits, jnp.int32))

    def rest(small, args):
        (here, ancestors, up_tab, low_tab, up_bufs, up_spill, low_send, low_spill, inverses, kid_parent) = args
        up_bufs = list(up_bufs)
        low_bufs = ring(low_send, rows)
        if not small:
            if up_spill is not None:
                up_bufs = up_bufs + ring(up_spill, rows)
            if low_spill is not None:
                low_bufs = low_bufs + ring(low_spill, rows)
        up_caps = (up.cap_w, up.cap_y) if small else (up.full_w, up.full_y)
        low_caps = (low.cap_w, low.cap_y) if small else (low.full_w, low.full_y)
        up_own, up_w = mult(up, *up_caps, here, up_tab, ancestors, up_bufs)
        up_other = other_half(up_own, cols)
        low_own, low_w = mult(low, *low_caps, here, low_tab, ancestors, low_bufs)
        low_other = other_half(low_own, cols)
        parent_cov, up_term = spread(up, up_tab, up_own, up_other, up_w)
        through, upper_part = cross(low, low_caps[1], low_tab, parent_cov, low_w)
        parent_diag = inverses[0] - total(up_term, rows, cols)
        upper_sum = total(upper_part, rows, cols)
        lead = low_w[: low.count]
        kid_diag = jnp.stack([lax.dynamic_index_in_dim(parent_diag, kid_parent[k], 0, False) for k in range(low.count)])
        upper = jnp.einsum("kxy,kyz->kxz", kid_diag, lead, precision=HIGH) + upper_sum
        diag = inverses[1] - jnp.einsum("kxy,kxz->kyz", lead, upper, precision=HIGH)
        child_cov, low_term = spread(low, low_tab, low_own, low_other, low_w, through)
        child_diag = diag - total(low_term, rows, cols)
        return parent_cov, parent_diag, child_cov, -upper, child_diag

    args = (
        here,
        ancestor_cov,
        up_tab,
        low_tab,
        tuple(up_bufs),
        up_spill,
        low_send,
        low_spill,
        (parent_inverse, child_inverse),
        child_parent,
    )
    return lax.cond(over, functools.partial(rest, False), functools.partial(rest, True), args)


def solution(mesh):
    in_specs = (
        P(("parts", "row"), "col", None, None),
        P("parts"),
        P(("parts", "sub"), None),
        P(("parts", "sub"), None, "row", None),
        P(("parts", "sub"), None, None),
        P(("parts", "sub")),
        P(("parts", "sub"), None),
        P(("parts", "sub"), None, "row", None),
        P(("parts", "sub"), None, None),
    )
    out_specs = (
        P(("parts", "sub"), "row", None, None),
        P(("parts", "sub"), None, None),
        P(("parts", "sub"), "row", None, None),
        P(("parts", "sub"), None, None),
        P(("parts", "sub"), None, None),
    )
    others = tuple((axis, mesh.shape[axis]) for axis in ("sub", "parts"))
    body = functools.partial(per_device, mesh.shape["row"], mesh.shape["col"], others)
    return jax.shard_map(body, mesh=mesh, in_specs=in_specs, out_specs=out_specs, check_vma=False)
```

time: 650 us -> 295 us (0.45)
  matrix products: 223 us -> 1.65 us
  waiting for transfers between devices: 326 us -> 180 us
  local copies, waits for them, and re-layouts: 73.5 us -> 12.5 us
  Pallas kernels: 0 us -> 56.4 us
  starting transfers between devices: 0.16 us -> 34.2 us
  between operations: 14.3 us -> 1.36 us
    psum x2 -> x0, waiting for transfers between devices: 239 us -> none  [the longest x1 180 us: per_device(): prod_one = lax.psum(partial_one, 'col')]
    dot_general x14 -> x2, matrix products: 223 us -> 1.65 us  [the longest x1 1 us: rest(): diag = inverses[1] - jnp.einsum('kxy,kxz->kyz', lead, upper, precision=HIGH)]
    ppermute x0 -> x34, waiting for transfers between devices: none -> 180 us  [shift(): return lax.ppermute(x, axis, [(i, (i + by) % size) for i in range(size)])]
    all_gather x2 -> x0, waiting for transfers between devices: 85.8 us -> none  [the longest x1 56 us: per_device(): lax.all_gather(child_factor, 'row', axis=2, tiled=True)]
    pallas_call x0 -> x7, Pallas kernels: none -> 56.4 us  [the longest x2 30.2 us: mult(): pl.pallas_call(functools.partial(mult_kernel, lay, pieces), out_shape=[ja...]
    unnamed x47 -> x18, local copies, waits for them, and re-layouts: 52.2 us -> 5.65 us
    ppermute x0 -> x34, starting transfers between devices: none -> 34.2 us  [shift(): return lax.ppermute(x, axis, [(i, (i + by) % size) for i in range(size)])]
    mul x1 -> x0, local copies, waits for them, and re-layouts: 7.27 us -> none  [per_device(): parent_cov = -mask_one[:, :, None, None] * prod_one]
  transfers between devices with their start and end apart: 4 -> 34, of which waited for: 4 -> 23; matrix products, arithmetic and copies ran while one was open for 23% -> 2% of each run, Pallas kernels for 0% -> 12%
where the time goes in v1:
time: 295 us; the launch traced here: 294 us
  waiting for transfers between devices  180 us (61%)
  Pallas kernels  56.4 us (19%)
  starting transfers between devices  34.2 us (12%)
  local copies, waits for them, and re-layouts  12.5 us (4%)
  loops' own time  4.29 us (1%)
  other arithmetic  3.5 us (1%)
    ppermute x34, waiting for transfers between devices, shift(): return lax.ppermute(x, axis, [(i, (i + by) % size) for i in range(size)])  180 us
    ppermute x34, starting transfers between devices, shift(): return lax.ppermute(x, axis, [(i, (i + by) % size) for i in range(size)])  34.2 us
    pallas_call x2, Pallas kernels, mult(): pl.pallas_call(functools.partial(mult_kernel, lay, pieces), out_shape=[ja...  30.2 us
    pallas_call x2, Pallas kernels, spread(): pl.pallas_call(functools.partial(spread_kernel, lay, add is not None), ou...  13.3 us
    pallas_call x2, Pallas kernels, plan(): pl.pallas_call(body, out_shape=outs, in_specs=[SMEM] * 5 + [HBM], out_spe...  7.07 us
  transfers between devices with their start and end apart: 34, of which 23 were waited for; matrix products, arithmetic and copies ran while one was open for 2% of the time, Pallas kernels for 12%

profile of v1, /device:TPU:0, one launch (start us, length us, event | category | flops | bytes accessed | tf_op | source)
XLA Modules:
  0.0 293.6 jit_solution(10806763083217930295)
XLA Ops:
  4.1 4.2 %shard_map.143 = (s32[660]{0:T(1024)S(1)}, s32[2]{0:T(128)S(1)}, f32[16,64,256]{2,1,0:T(8,128)S(1)}, f32[8,64,256]{2,1,0:T(8,128)}) custom-call(s32[2]{0:T(128)S(1)} %pad_add_fusion.refs_0_, s32[32]{0:T(128)S(1)} %copy-done.6, s32[2,12]{1,0:T(2,128)S(1)} %copy-done.4, s32[2]{0:T(128)} %refs_3_.3, s32[2,8]{1,0:T(2,128)S(1)} %copy-done.5, ...), custom_call_target="tpu_custom_call" | custom-call | tf_op jit(solution)/shard_map/pallas_call | solution.py:150
  8.3 3.1 %collective-permute-start.66 = (f32[16,64,256]{2,1,0:T(8,128)S(1)}, f32[16,64,256]{2,1,0:T(8,128)S(1)}, u32[]{:S(2)}, u32[]{:S(2)}) collective-permute-start(f32[16,64,256]{2,1,0:T(8,128)S(1)} %get-tuple-element.114), channel_id=1, source_target_pairs={{0,4},{4,8},{8,12},{12,0},{1,5},{5,9},{9,13},{13,1},{2,6},{6,10},{... | collective-permute-start | bytes 3145736 | tf_op jit(solution)/shard_map/ppermute | solution.py:329
  11.4 25.3 %collective-permute-done.66 = f32[16,64,256]{2,1,0:T(8,128)S(1)} collective-permute-done((f32[16,64,256]{2,1,0:T(8,128)S(1)}, f32[16,64,256]{2,1,0:T(8,128)S(1)}, u32[]{:S(2)}, u32[]{:S(2)}) %collective-permute-start.66) | collective-permute-done | bytes 1048608 | tf_op jit(solution)/shard_map/ppermute | solution.py:329
  36.7 26.4 %collective-permute-done.67 = f32[16,64,256]{2,1,0:T(8,128)S(1)} collective-permute-done((f32[16,64,256]{2,1,0:T(8,128)S(1)}, f32[16,64,256]{2,1,0:T(8,128)S(1)}, u32[]{:S(2)}, u32[]{:S(2)}) %collective-permute-start.67) | collective-permute-done | bytes 1048608 | tf_op jit(solution)/shard_map/ppermute | solution.py:329
  64.3 2.9 shard_map.144
  74.0 14.5 %collective-permute-done.68 = f32[16,64,256]{2,1,0:T(8,128)S(1)} collective-permute-done((f32[16,64,256]{2,1,0:T(8,128)S(1)}, f32[16,64,256]{2,1,0:T(8,128)S(1)}, u32[]{:S(2)}, u32[]{:S(2)}) %collective-permute-start.68) | collective-permute-done | bytes 1048608 | tf_op jit(solution)/shard_map/ppermute | solution.py:329
  88.5 204.1 %conditional.1 = (f32[2,8,256,256]{3,2,1,0:T(8,128)}, f32[2,8,256,256]{3,2,1,0:T(8,128)}, f32[2,256,256]{2,1,0:T(8,128)}, f32[2,256,256]{2,1,0:T(8,128)S(1)}, f32[2,256,256]{2,1,0:T(8,128)S(1)}) conditional(s32[]{:T(128)} %convert_element_type.3, (s32[2]{0:T(128)S(1)}, s32[660]{0:T(1024)S(1)}, f32[8,16,256,256]{3,2,1,0:T(8,128)}, ...), branch_computations={%region_1.2_spmd, %region_2.3_spmd} | conditional | flops 5807223296 | bytes 212412064 | solution.py:434
  89.9 16.8 %branch_0_fun.5 = (f32[10,256,256]{2,1,0:T(8,128)S(1)}, f32[16,256,256]{2,1,0:T(8,128)}) custom-call(s32[2]{0:T(128)S(1)} %get-tuple-element.53.here, s32[660]{0:T(1024)S(1)} %get-tuple-element.52.tab, f32[8,16,256,256]{3,2,1,0:T(8,128)} %get-tuple-element.54.ancestors, f32[16,64,256]{2,1,0:T(8,128)} %get-tuple-element.55.refs_0_, ...), custom_call_target="tpu_custom_call" | custom-call | flops 1000000000 | bytes 20000000 | tf_op jit(solution)/shard_map/cond/branch_0_fun/pallas_call | solution.py:231
  106.9 23.2 %collective-permute-done.9.refs_1_ = f32[14,64,256]{2,1,0:T(8,128)S(1)} collective-permute-done((f32[14,64,256]{2,1,0:T(8,128)S(1)}, f32[14,64,256]{2,1,0:T(8,128)S(1)}, u32[]{:S(2)}, u32[]{:S(2)}) %collective-permute-start.9) | collective-permute-done | bytes 917536 | tf_op jit(solution)/shard_map/cond/branch_0_fun/ppermute | solution.py:329
  130.1 22.4 %collective-permute-done.10.refs_2_ = f32[14,64,256]{2,1,0:T(8,128)} collective-permute-done((f32[14,64,256]{2,1,0:T(8,128)S(1)}, f32[14,64,256]{2,1,0:T(8,128)}, u32[]{:S(2)}, u32[]{:S(2)}) %collective-permute-start.10) | collective-permute-done | bytes 917536 | tf_op jit(solution)/shard_map/cond/branch_0_fun/ppermute | solution.py:329
  152.5 11.7 %collective-permute-done.other = f32[10,256,256]{2,1,0:T(8,128)} collective-permute-done((f32[10,256,256]{2,1,0:T(8,128)S(1)}, f32[10,256,256]{2,1,0:T(8,128)}, u32[]{:S(2)}, u32[]{:S(2)}) %collective-permute-start) | collective-permute-done | bytes 2621472 | tf_op jit(solution)/shard_map/cond/branch_0_fun/ppermute | solution.py:329
  164.2 5.5 %branch_0_fun.6 = (f32[2,8,256,256]{3,2,1,0:T(8,128)S(1)}, f32[2,256,256]{2,1,0:T(8,128)S(1)}) custom-call(s32[660]{0:T(1024)S(1)} %get-tuple-element.52.tab, f32[10,256,256]{2,1,0:T(8,128)S(1)} %get-tuple-element.59.own, f32[10,256,256]{2,1,0:T(8,128)} %collective-permute-done.other, f32[16,256,256]{2,1,0:T(8,128)} %get-tuple-element.60.w), custom_call_target="tpu_custom_call" | custom-call | flops 1000000000 | bytes 10000000 | tf_op jit(solution)/shard_map/cond/branch_0_fun/pallas_call | solution.py:282
  169.8 4.4 %collective-permute-done.11.refs_3_ = f32[14,64,256]{2,1,0:T(8,128)} collective-permute-done((f32[14,64,256]{2,1,0:T(8,128)}, f32[14,64,256]{2,1,0:T(8,128)}, u32[]{:S(2)}, u32[]{:S(2)}) %collective-permute-start.11) | collective-permute-done | bytes 917536 | tf_op jit(solution)/shard_map/cond/branch_0_fun/ppermute | solution.py:329
  174.3 13.4 %branch_0_fun.7 = (f32[8,256,256]{2,1,0:T(8,128)}, f32[14,256,256]{2,1,0:T(8,128)}) custom-call(s32[2]{0:T(128)S(1)} %get-tuple-element.53.here, s32[468]{0:T(512)S(1)} %get-tuple-element.64.tab, f32[8,16,256,256]{3,2,1,0:T(8,128)} %get-tuple-element.54.ancestors, f32[14,64,256]{2,1,0:T(8,128)S(1)} %copy-done.16, ...), custom_call_target="tpu_custom_call" | custom-call | flops 1000000000 | bytes 20000000 | tf_op jit(solution)/shard_map/cond/branch_0_fun/pallas_call | solution.py:231
  187.7 5.8 %branch_0_fun.8 = (f32[8,256,256]{2,1,0:T(8,128)S(1)}, f32[2,256,256]{2,1,0:T(8,128)S(1)}) custom-call(s32[468]{0:T(512)S(1)} %get-tuple-element.64.tab, f32[2,8,256,256]{3,2,1,0:T(8,128)S(1)} %get-tuple-element.164.cov, f32[14,256,256]{2,1,0:T(8,128)} %get-tuple-element.67.w), custom_call_target="tpu_custom_call" | custom-call | flops 1000000000 | bytes 10000000 | tf_op jit(solution)/shard_map/cond/branch_0_fun/pallas_call | solution.py:315
  195.6 3.8 %collective-permute-start.4 = (f32[64,256]{1,0:T(8,128)}, f32[64,256]{1,0:T(8,128)}, u32[]{:S(2)}, u32[]{:S(2)}) collective-permute-start(f32[64,256]{1,0:T(8,128)} %get-tuple-element.137), channel_id=1, source_target_pairs={{0,12},{4,0},{8,4},{12,8},{1,13},{5,1},{9,5},{13,9},{2,14},{6,2},{... | collective-permute-start | bytes 196616 | tf_op jit(solution)/shard_map/cond/branch_0_fun/ppermute | solution.py:329
  217.2 3.3 %collective-permute-done.15 = f32[64,256]{1,0:T(8,128)S(1)} collective-permute-done((f32[64,256]{1,0:T(8,128)S(1)}, f32[64,256]{1,0:T(8,128)S(1)}, u32[]{:S(2)}, u32[]{:S(2)}) %collective-permute-start.15) | collective-permute-done | bytes 65568 | tf_op jit(solution)/shard_map/cond/branch_0_fun/ppermute | solution.py:329
  225.6 4.6 %collective-permute-done.18 = f32[64,256]{1,0:T(8,128)S(1)} collective-permute-done((f32[64,256]{1,0:T(8,128)S(1)}, f32[64,256]{1,0:T(8,128)S(1)}, u32[]{:S(2)}, u32[]{:S(2)}) %collective-permute-start.18) | collective-permute-done | bytes 65568 | tf_op jit(solution)/shard_map/cond/branch_0_fun/ppermute | solution.py:329
  231.6 20.2 %collective-permute-done.12.other = f32[8,256,256]{2,1,0:T(8,128)S(1)} collective-permute-done((f32[8,256,256]{2,1,0:T(8,128)S(1)}, f32[8,256,256]{2,1,0:T(8,128)S(1)}, u32[]{:S(2)}, u32[]{:S(2)}) %collective-permute-start.12) | collective-permute-done | bytes 2097184 | tf_op jit(solution)/shard_map/cond/branch_0_fun/ppermute | solution.py:329
  253.2 7.9 %branch_0_fun.9 = (f32[2,8,256,256]{3,2,1,0:T(8,128)}, f32[2,256,256]{2,1,0:T(8,128)S(1)}) custom-call(s32[468]{0:T(512)S(1)} %get-tuple-element.64.tab, f32[8,256,256]{2,1,0:T(8,128)S(1)} %copy-done, f32[8,256,256]{2,1,0:T(8,128)} %copy-done.21, f32[14,256,256]{2,1,0:T(8,128)} %get-tuple-element.67.w, f32[8,256,256]{2,1,0:T(8,128)} %copy-done.1), custom_call_target="tpu_custom_call" | custom-call | flops 1000000000 | bytes 10000000 | tf_op jit(solution)/shard_map/cond/branch_0_fun/pallas_call | solution.py:282
  262.1 5.4 %collective-permute-done.21 = f32[256,256]{1,0:T(8,128)S(1)} collective-permute-done((f32[256,256]{1,0:T(8,128)S(1)}, f32[256,256]{1,0:T(8,128)S(1)}, u32[]{:S(2)}, u32[]{:S(2)}) %collective-permute-start.21) | collective-permute-done | bytes 262176 | tf_op jit(solution)/shard_map/cond/branch_0_fun/ppermute | solution.py:329
  274.5 4.1 %collective-permute-start.25 = (f32[64,256]{1,0:T(8,128)S(1)}, f32[64,256]{1,0:T(8,128)S(1)}, u32[]{:S(2)}, u32[]{:S(2)}) collective-permute-start(f32[64,256]{1,0:T(8,128)S(1)} %fusion.6), channel_id=1, source_target_pairs={{0,12},{4,0},{8,4},{12,8},{1,13},{5,1},{9,5},{13,9},{2,14},{6,2},{... | collective-permute-start | bytes 196616 | tf_op jit(solution)/shard_map/cond/branch_0_fun/ppermute | solution.py:329
  280.5 3.4 %collective-permute-done.26 = f32[64,256]{1,0:T(8,128)S(1)} collective-permute-done((f32[64,256]{1,0:T(8,128)S(1)}, f32[64,256]{1,0:T(8,128)S(1)}, u32[]{:S(2)}, u32[]{:S(2)}) %collective-permute-start.26) | collective-permute-done | bytes 65568 | tf_op jit(solution)/shard_map/cond/branch_0_fun/ppermute | solution.py:329
  287.7 3.7 %collective-permute-done.28 = f32[256,256]{1,0:T(8,128)S(1)} collective-permute-done((f32[256,256]{1,0:T(8,128)S(1)}, f32[256,256]{1,0:T(8,128)S(1)}, u32[]{:S(2)}, u32[]{:S(2)}) %collective-permute-start.28) | collective-permute-done | bytes 262176 | tf_op jit(solution)/shard_map/cond/branch_0_fun/ppermute | solution.py:329
  (145 shorter events, 52.1 us)
Async XLA Ops:
  8.3 28.4 %collective-permute-start.66 = (f32[16,64,256]{2,1,0:T(8,128)S(1)}, f32[16,64,256]{2,1,0:T(8,128)S(1)}, u32[]{:S(2)}, u32[]{:S(2)}) collective-permute-start(f32[16,64,256]{2,1,0:T(8,128)S(1)} %get-tuple-element.114), channel_id=1, source_target_pairs={{0,4},{4,8},{8,12},{12,0},{1,5},{5,9},{9,13},{13,1},{2,6},{6,10},{... | collective-permute-start | bytes 3145736 | tf_op jit(solution)/shard_map/ppermute | solution.py:329
  36.7 26.4 %collective-permute-start.67 = (f32[16,64,256]{2,1,0:T(8,128)S(1)}, f32[16,64,256]{2,1,0:T(8,128)S(1)}, u32[]{:S(2)}, u32[]{:S(2)}) collective-permute-start(f32[16,64,256]{2,1,0:T(8,128)S(1)} %collective-permute-done.66), channel_id=1, source_target_pairs={{0,4},{4,8},{8,12},{12,0},{1,5},{5,9},{9,13},{13,1},{2,6},{6,10},{... | collective-permute-start | bytes 3145736 | tf_op jit(solution)/shard_map/ppermute | solution.py:329
  63.1 25.5 %collective-permute-start.68 = (f32[16,64,256]{2,1,0:T(8,128)S(1)}, f32[16,64,256]{2,1,0:T(8,128)S(1)}, u32[]{:S(2)}, u32[]{:S(2)}) collective-permute-start(f32[16,64,256]{2,1,0:T(8,128)S(1)} %collective-permute-done.67), channel_id=1, source_target_pairs={{0,4},{4,8},{8,12},{12,0},{1,5},{5,9},{9,13},{13,1},{2,6},{6,10},{... | collective-permute-start | bytes 3145736 | tf_op jit(solution)/shard_map/ppermute | solution.py:329
  106.7 57.5 %collective-permute-start = (f32[10,256,256]{2,1,0:T(8,128)S(1)}, f32[10,256,256]{2,1,0:T(8,128)}, u32[]{:S(2)}, u32[]{:S(2)}) collective-permute-start(f32[10,256,256]{2,1,0:T(8,128)S(1)} %get-tuple-element.59.own), channel_id=1, source_target_pairs={{0,2},{2,0},{1,3},{3,1},{4,6},{6,4},{5,7},{7,5},{8,10},{10,8},{9,1... | collective-permute-start | bytes 7864328 | tf_op jit(solution)/shard_map/cond/branch_0_fun/ppermute | solution.py:329
  106.8 23.3 %collective-permute-start.9 = (f32[14,64,256]{2,1,0:T(8,128)S(1)}, f32[14,64,256]{2,1,0:T(8,128)S(1)}, u32[]{:S(2)}, u32[]{:S(2)}) collective-permute-start(f32[14,64,256]{2,1,0:T(8,128)S(1)} %copy-done.15), channel_id=1, source_target_pairs={{0,4},{4,8},{8,12},{12,0},{1,5},{5,9},{9,13},{13,1},{2,6},{6,10},{... | collective-permute-start | bytes 2752520 | tf_op jit(solution)/shard_map/cond/branch_0_fun/ppermute | solution.py:329
  130.1 22.4 %collective-permute-start.10 = (f32[14,64,256]{2,1,0:T(8,128)S(1)}, f32[14,64,256]{2,1,0:T(8,128)}, u32[]{:S(2)}, u32[]{:S(2)}) collective-permute-start(f32[14,64,256]{2,1,0:T(8,128)S(1)} %collective-permute-done.9.refs_1_), channel_id=1, source_target_pairs={{0,4},{4,8},{8,12},{12,0},{1,5},{5,9},{9,13},{13,1},{2,6},{6,10},{... | collective-permute-start | bytes 2752520 | tf_op jit(solution)/shard_map/cond/branch_0_fun/ppermute | solution.py:329
  152.5 21.7 %collective-permute-start.11 = (f32[14,64,256]{2,1,0:T(8,128)}, f32[14,64,256]{2,1,0:T(8,128)}, u32[]{:S(2)}, u32[]{:S(2)}) collective-permute-start(f32[14,64,256]{2,1,0:T(8,128)} %collective-permute-done.10.refs_2_), channel_id=1, source_target_pairs={{0,4},{4,8},{8,12},{12,0},{1,5},{5,9},{9,13},{13,1},{2,6},{6,10},{... | collective-permute-start | bytes 2752520 | tf_op jit(solution)/shard_map/cond/branch_0_fun/ppermute | solution.py:329
  169.7 25.2 %collective-permute-start.1 = (f32[256,256]{1,0:T(8,128)S(1)}, f32[256,256]{1,0:T(8,128)S(1)}, u32[]{:S(2)}, u32[]{:S(2)}) collective-permute-start(f32[256,256]{1,0:T(8,128)S(1)} %dynamic-slice_bitcast_fusion.2), channel_id=1, source_target_pairs={{0,2},{2,0},{1,3},{3,1},{4,6},{6,4},{5,7},{7,5},{8,10},{10,8},{9,1... | collective-permute-start | bytes 786440 | tf_op jit(solution)/shard_map/cond/branch_0_fun/ppermute | solution.py:329
  194.8 15.9 %collective-permute-start.13 = (f32[256,256]{1,0:T(8,128)S(1)}, f32[256,256]{1,0:T(8,128)S(1)}, u32[]{:S(2)}, u32[]{:S(2)}) collective-permute-start(f32[256,256]{1,0:T(8,128)S(1)} %dynamic-slice_bitcast_fusion.1), channel_id=1, source_target_pairs={{0,2},{2,0},{1,3},{3,1},{4,6},{6,4},{5,7},{7,5},{8,10},{10,8},{9,1... | collective-permute-start | bytes 786440 | tf_op jit(solution)/shard_map/cond/branch_0_fun/ppermute | solution.py:329
  195.6 10.1 %collective-permute-start.2 = (f32[64,256]{1,0:T(8,128)}, f32[64,256]{1,0:T(8,128)S(1)}, u32[]{:S(2)}, u32[]{:S(2)}) collective-permute-start(f32[64,256]{1,0:T(8,128)} %get-tuple-element.136), channel_id=1, source_target_pairs={{0,4},{4,8},{8,12},{12,0},{1,5},{5,9},{9,13},{13,1},{2,6},{6,10},{... | collective-permute-start | bytes 196616 | tf_op jit(solution)/shard_map/cond/branch_0_fun/ppermute | solution.py:329
  195.6 10.1 %collective-permute-start.3 = (f32[64,256]{1,0:T(8,128)}, f32[64,256]{1,0:T(8,128)S(1)}, u32[]{:S(2)}, u32[]{:S(2)}) collective-permute-start(f32[64,256]{1,0:T(8,128)} %get-tuple-element.138), channel_id=1, source_target_pairs={{0,8},{4,12},{8,0},{12,4},{1,9},{5,13},{9,1},{13,5},{2,10},{6,14},... | collective-permute-start | bytes 196616 | tf_op jit(solution)/shard_map/cond/branch_0_fun/ppermute | solution.py:329
  195.6 10.1 %collective-permute-start.4 = (f32[64,256]{1,0:T(8,128)}, f32[64,256]{1,0:T(8,128)}, u32[]{:S(2)}, u32[]{:S(2)}) collective-permute-start(f32[64,256]{1,0:T(8,128)} %get-tuple-element.137), channel_id=1, source_target_pairs={{0,12},{4,0},{8,4},{12,8},{1,13},{5,1},{9,5},{13,9},{2,14},{6,2},{... | collective-permute-start | bytes 196616 | tf_op jit(solution)/shard_map/cond/branch_0_fun/ppermute | solution.py:329
  203.7 48.1 %collective-permute-start.12 = (f32[8,256,256]{2,1,0:T(8,128)S(1)}, f32[8,256,256]{2,1,0:T(8,128)S(1)}, u32[]{:S(2)}, u32[]{:S(2)}) collective-permute-start(f32[8,256,256]{2,1,0:T(8,128)S(1)} %copy-done), channel_id=1, source_target_pairs={{0,2},{2,0},{1,3},{3,1},{4,6},{6,4},{5,7},{7,5},{8,10},{10,8},{9,1... | collective-permute-start | bytes 6291464 | tf_op jit(solution)/shard_map/cond/branch_0_fun/ppermute | solution.py:329
  208.4 6.8 %collective-permute-start.6 = (f32[64,256]{1,0:T(8,128)S(1)}, f32[64,256]{1,0:T(8,128)S(1)}, u32[]{:S(2)}, u32[]{:S(2)}) collective-permute-start(f32[64,256]{1,0:T(8,128)S(1)} %fusion.10), channel_id=1, source_target_pairs={{0,8},{4,12},{8,0},{12,4},{1,9},{5,13},{9,1},{13,5},{2,10},{6,14},... | collective-permute-start | bytes 196616 | tf_op jit(solution)/shard_map/cond/branch_0_fun/ppermute | solution.py:329
  208.8 7.1 %collective-permute-start.7 = (f32[64,256]{1,0:T(8,128)S(1)}, f32[64,256]{1,0:T(8,128)S(1)}, u32[]{:S(2)}, u32[]{:S(2)}) collective-permute-start(f32[64,256]{1,0:T(8,128)S(1)} %fusion.10), channel_id=1, source_target_pairs={{0,4},{4,8},{8,12},{12,0},{1,5},{5,9},{9,13},{13,1},{2,6},{6,10},{... | collective-permute-start | bytes 196616 | tf_op jit(solution)/shard_map/cond/branch_0_fun/ppermute | solution.py:329
  210.8 6.4 %collective-permute-start.14 = (f32[64,256]{1,0:T(8,128)S(1)}, f32[64,256]{1,0:T(8,128)S(1)}, u32[]{:S(2)}, u32[]{:S(2)}) collective-permute-start(f32[64,256]{1,0:T(8,128)S(1)} %get-tuple-element.133), channel_id=1, source_target_pairs={{0,4},{4,8},{8,12},{12,0},{1,5},{5,9},{9,13},{13,1},{2,6},{6,10},{... | collective-permute-start | bytes 196616 | tf_op jit(solution)/shard_map/cond/branch_0_fun/ppermute | solution.py:329
  212.0 8.5 %collective-permute-start.15 = (f32[64,256]{1,0:T(8,128)S(1)}, f32[64,256]{1,0:T(8,128)S(1)}, u32[]{:S(2)}, u32[]{:S(2)}) collective-permute-start(f32[64,256]{1,0:T(8,128)S(1)} %get-tuple-element.135), channel_id=1, source_target_pairs={{0,8},{4,12},{8,0},{12,4},{1,9},{5,13},{9,1},{13,5},{2,10},{6,14},... | collective-permute-start | bytes 196616 | tf_op jit(solution)/shard_map/cond/branch_0_fun/ppermute | solution.py:329
  222.2 39.0 %collective-permute-start.8 = (f32[256,256]{1,0:T(8,128)S(1)}, f32[256,256]{1,0:T(8,128)S(1)}, u32[]{:S(2)}, u32[]{:S(2)}) collective-permute-start(f32[256,256]{1,0:T(8,128)S(1)} %bitcast.229), channel_id=1, source_target_pairs={{0,2},{2,0},{1,3},{3,1},{4,6},{6,4},{5,7},{7,5},{8,10},{10,8},{9,1... | collective-permute-start | bytes 786440 | tf_op jit(solution)/shard_map/cond/branch_0_fun/ppermute | solution.py:329
  225.0 6.1 %collective-permute-start.19 = (f32[64,256]{1,0:T(8,128)S(1)}, f32[64,256]{1,0:T(8,128)S(1)}, u32[]{:S(2)}, u32[]{:S(2)}) collective-permute-start(f32[64,256]{1,0:T(8,128)S(1)} %fusion.8), channel_id=1, source_target_pairs={{0,4},{4,8},{8,12},{12,0},{1,5},{5,9},{9,13},{13,1},{2,6},{6,10},{... | collective-permute-start | bytes 196616 | tf_op jit(solution)/shard_map/cond/branch_0_fun/ppermute | solution.py:329
  231.2 47.3 %collective-permute-start.20 = (f32[256,256]{1,0:T(8,128)S(1)}, f32[256,256]{1,0:T(8,128)S(1)}, u32[]{:S(2)}, u32[]{:S(2)}) collective-permute-start(f32[256,256]{1,0:T(8,128)S(1)} %bitcast.226), channel_id=1, source_target_pairs={{0,2},{2,0},{1,3},{3,1},{4,6},{6,4},{5,7},{7,5},{8,10},{10,8},{9,1... | collective-permute-start | bytes 786440 | tf_op jit(solution)/shard_map/cond/branch_0_fun/ppermute | solution.py:329
  261.1 6.4 %collective-permute-start.21 = (f32[256,256]{1,0:T(8,128)S(1)}, f32[256,256]{1,0:T(8,128)S(1)}, u32[]{:S(2)}, u32[]{:S(2)}) collective-permute-start(f32[256,256]{1,0:T(8,128)S(1)} %dynamic-slice_bitcast_fusion), channel_id=1, source_target_pairs={{0,2},{2,0},{1,3},{3,1},{4,6},{6,4},{5,7},{7,5},{8,10},{10,8},{9,1... | collective-permute-start | bytes 786440 | tf_op jit(solution)/shard_map/cond/branch_0_fun/ppermute | solution.py:329
  267.6 6.1 %collective-permute-start.22 = (f32[64,256]{1,0:T(8,128)S(1)}, f32[64,256]{1,0:T(8,128)S(1)}, u32[]{:S(2)}, u32[]{:S(2)}) collective-permute-start(f32[64,256]{1,0:T(8,128)S(1)} %get-tuple-element.130), channel_id=1, source_target_pairs={{0,4},{4,8},{8,12},{12,0},{1,5},{5,9},{9,13},{13,1},{2,6},{6,10},{... | collective-permute-start | bytes 196616 | tf_op jit(solution)/shard_map/cond/branch_0_fun/ppermute | solution.py:329
  278.7 6.1 %collective-permute-start.27 = (f32[64,256]{1,0:T(8,128)S(1)}, f32[64,256]{1,0:T(8,128)S(1)}, u32[]{:S(2)}, u32[]{:S(2)}) collective-permute-start(f32[64,256]{1,0:T(8,128)S(1)} %fusion.6), channel_id=1, source_target_pairs={{0,4},{4,8},{8,12},{12,0},{1,5},{5,9},{9,13},{13,1},{2,6},{6,10},{... | collective-permute-start | bytes 196616 | tf_op jit(solution)/shard_map/cond/branch_0_fun/ppermute | solution.py:329
  284.9 6.4 %collective-permute-start.28 = (f32[256,256]{1,0:T(8,128)S(1)}, f32[256,256]{1,0:T(8,128)S(1)}, u32[]{:S(2)}, u32[]{:S(2)}) collective-permute-start(f32[256,256]{1,0:T(8,128)S(1)} %bitcast.242), channel_id=1, source_target_pairs={{0,2},{2,0},{1,3},{3,1},{4,6},{6,4},{5,7},{7,5},{8,10},{10,8},{9,1... | collective-permute-start | bytes 786440 | tf_op jit(solution)/shard_map/cond/branch_0_fun/ppermute | solution.py:329
  (31 other events, 276.3 us)
